TPU v7x, 512 devices: a whole 4x4x16 slice. The times are simulated.
512 devices in a mesh: section: 4 (over x), seq: 128 (over z, y, core).
Axes of the slice: x: 4, y: 4, z: 16, core: 2. Of those that a mesh axis runs over, the one named last changes fastest.
Arguments:
- feats: bfloat16 [4096, 8, 8, 768], P(('section', 'seq'))
- dw_weight: float32 [7, 7, 768], replicated, may hold values from -0.875 to 0.875
- dw_bias: float32 [768], replicated, may hold values from -3 to 3
- ln1_gain: float32 [768], replicated, may hold values from 0.5 to 2
- w_up: bfloat16 [1536, 768], P('section'), may hold values from -0.21875 to 0.21875
- b_up: bfloat16 [1536], P('section'), may hold values from -3 to 3
- w_down: bfloat16 [1536, 768], P('section'), may hold values from -0.15625 to 0.15625
- b_down: float32 [768], replicated, may hold values from -3 to 3
- layer_scale: float32 [768], replicated, may hold values from 0.3 to 1.5
- lnf_gain: float32 [768], replicated, may hold values from 0.5 to 2
- w_head: bfloat16 [768, 1536], P(None, 'section'), may hold values from -0.21875 to 0.21875
- prior: bfloat16 [77824, 1536], P(('section', 'seq')), may hold values from -6 to 6
- counts: int32 [512], P(('section', 'seq')), may hold values from 0 to 152, as said below
- positions: int32 [81920], P(('section', 'seq')), may hold values from 0 to 32767, as said below
- w_in: bfloat16 [1536, 768], P('section')
- ln_gain: float32 [768], replicated, may hold values from 0.5 to 2
- w_qkv: bfloat16 [768, 2304], P(None, 'section'), may hold values from -0.21875 to 0.21875
- qn_gain: float32 [64], replicated, may hold values from 0.5 to 2
- kn_gain: float32 [64], replicated, may hold values from 0.5 to 2
- offsets: int32 [12], replicated, may hold values from 0 to 15
- w_out: bfloat16 [768, 768], P('section'), may hold values from -6 to 6
Outputs:
- slide_out: bfloat16 [32768, 768], P('seq', 'section')
Inputs may be any that keep to these rules, and one draw needn't show every extreme that they name: `counts`: slot k of a device is valid when k < 8 + its count. Some device of every section index has count 152. `positions`: only valid slots' entries count. The valid slots of all devices hold every position 0 to 32767 exactly once; a valid slot of a device with section index s holds a position p with (p mod 256) div (64) = s. At most 2 valid slots of one device have the same p div 256, and some device reaches 2.
All inputs are finite; a program needn't handle non-finite values.
Results may differ from a plain program's by a relative error of at most 0.014.
Values may be sent and summed in bfloat16 or wider, within the bound.
No kernel may reach another device: no remote copies, remote signals or barrier semaphores. Data moves between devices by JAX's collectives and lax.ppermute only.
A program may use at most 64 MiB of HBM per device.

v0:
```python
import math
import jax
import jax.numpy as jnp
from jax import lax
from jax.sharding import PartitionSpec as P

HS = 64
RB = 16
ROWS = 256


def layer_norm(values, gain_vec):
    row_mean = jnp.mean(values, axis=-1, keepdims=True)
    centered = values - row_mean
    variance = jnp.mean(centered * centered, axis=-1, keepdims=True)
    return centered * lax.rsqrt(variance + 1e-06) * gain_vec


def rms_scale(values, gain_vec):
    return values * lax.rsqrt(jnp.mean(values * values, axis=-1, keepdims=True) + 1e-06) * gain_vec


def conv_norm(tile_maps, dw_weight, dw_bias, ln1_gain):
    map_side = tile_maps.shape[1]
    kernel = dw_weight.shape[0]
    half_width = (kernel - 1) // 2
    source = tile_maps.astype(jnp.float32)
    padded = jnp.pad(source, ((0, 0), (half_width, half_width), (half_width, half_width), (0, 0)))
    conv_sum = jnp.zeros_like(source) + dw_bias
    for row_off in range(kernel):
        for col_off in range(kernel):
            conv_sum = (
                conv_sum
                + padded[:, row_off : row_off + map_side, col_off : col_off + map_side, :]
                * dw_weight[row_off, col_off]
            )
    channels = source.shape[-1]
    normed_maps = layer_norm(conv_sum, ln1_gain).astype(jnp.bfloat16).reshape(-1, channels)
    return (source, normed_maps)


def pointwise(maps, up_rows, up_bias, down_rows, pixels):
    pre_act = lax.dot_general(
        maps, up_rows, (((1,), (1,)), ((), ())), preferred_element_type=jnp.float32
    ) + up_bias.astype(jnp.float32)
    hidden = jax.nn.gelu(pre_act, approximate=False).astype(jnp.bfloat16)
    branch = jnp.dot(hidden, down_rows, preferred_element_type=jnp.float32)
    return jnp.mean(branch.reshape(maps.shape[0] // pixels, pixels, branch.shape[1]), axis=1)


def shards(
    feats,
    dw_weight,
    dw_bias,
    ln1_gain,
    w_up,
    b_up,
    w_down,
    b_down,
    layer_scale,
    lnf_gain,
    w_head,
    prior,
    counts,
    positions,
    w_in,
    ln_gain,
    w_qkv,
    qn_gain,
    kn_gain,
    offsets,
    w_out,
):
    n_seq = lax.axis_size("seq")
    n_section = lax.axis_size("section")
    section_idx = lax.axis_index("section")
    pixels = feats.shape[1] * feats.shape[2]
    source, normed_maps = conv_norm(feats, dw_weight, dw_bias, ln1_gain)
    up_all, bias_all, down_all, head_all, in_all = (
        lax.all_gather(w_up, "section", axis=0, tiled=True),
        lax.all_gather(b_up, "section", axis=0, tiled=True),
        lax.all_gather(w_down, "section", axis=0, tiled=True),
        lax.all_gather(w_head, "section", axis=1, tiled=True),
        lax.all_gather(w_in, "section", axis=0, tiled=True),
    )
    branch_pooled = pointwise(normed_maps, up_all, bias_all, down_all, pixels)
    pooled = jnp.mean(source, axis=(1, 2)) + layer_scale * (branch_pooled + b_down)
    feature = layer_norm(pooled, lnf_gain).astype(jnp.bfloat16)
    fresh_emb = jnp.dot(feature, head_all, preferred_element_type=jnp.float32).astype(jnp.bfloat16)
    slot_rows = jnp.concatenate([fresh_emb, prior], axis=0)
    slot_total = slot_rows.shape[0]
    q_rows = ROWS // n_section
    capacity = -(-slot_total // n_seq)
    live_mask = jnp.arange(slot_total) < feats.shape[0] + counts[0]
    dest_shard = positions // ROWS
    row_in = positions % ROWS - section_idx * q_rows
    onehot_dest = jnp.logical_and(
        live_mask[:, None], dest_shard[:, None] == jnp.arange(n_seq)[None, :]
    ).astype(jnp.int32)
    before = jnp.cumsum(onehot_dest, axis=0) - onehot_dest
    within = jnp.sum(before * onehot_dest, axis=1)
    bucket = jnp.where(live_mask, dest_shard * capacity + within, -1)
    select = jnp.arange(n_seq * capacity)[:, None] == bucket[None, :]
    send_rows = (jnp.sum(jnp.where(select, row_in[None, :] + 1, 0), axis=1) - 1).reshape(
        n_seq, capacity
    )
    select_mat = select.astype(jnp.bfloat16)
    got_vals = lax.all_to_all(
        jnp.dot(select_mat, slot_rows, preferred_element_type=jnp.float32)
        .astype(jnp.bfloat16)
        .reshape(n_seq, capacity, slot_rows.shape[1]),
        "seq",
        split_axis=0,
        concat_axis=0,
        tiled=True,
    )
    got_rows = lax.all_to_all(send_rows, "seq", split_axis=0, concat_axis=0, tiled=True)
    flat_rows = got_rows.reshape(-1)
    placer = (jnp.arange(q_rows)[:, None] == flat_rows[None, :]).astype(jnp.bfloat16)
    x_local = jnp.dot(
        jnp.dot(
            placer,
            got_vals.reshape(flat_rows.shape[0], got_vals.shape[2]),
            preferred_element_type=jnp.float32,
        ).astype(jnp.bfloat16),
        in_all,
        preferred_element_type=jnp.float32,
    ).astype(jnp.bfloat16)
    x_rows = lax.all_gather(x_local, "section", axis=0, tiled=True)
    rows_total = x_rows.shape[0]
    normed = layer_norm(x_rows.astype(jnp.float32), ln_gain).astype(jnp.bfloat16)
    heads_here = w_qkv.shape[1] // (3 * HS)
    qkv_rows = (
        jnp.dot(normed, w_qkv, preferred_element_type=jnp.float32)
        .astype(jnp.bfloat16)
        .reshape(rows_total, 3, heads_here, HS)
    )
    queries = rms_scale(qkv_rows[:, 0].astype(jnp.float32), qn_gain).astype(jnp.bfloat16)
    keys_here = rms_scale(qkv_rows[:, 1].astype(jnp.float32), kn_gain).astype(jnp.bfloat16)
    values_here = qkv_rows[:, 2]
    score_scale = 1.0 / math.sqrt(HS)
    scores = (
        jnp.einsum("qhd,khd->hqk", queries, keys_here, preferred_element_type=jnp.float32)
        * score_scale
    )
    weights = jnp.exp(scores)
    local_den = jnp.sum(weights, axis=-1)
    local_num = jnp.einsum(
        "hqk,khd->hqd",
        weights.astype(jnp.bfloat16),
        values_here,
        preferred_element_type=jnp.float32,
    )
    my_offsets = lax.dynamic_slice_in_dim(offsets, section_idx * heads_here, heads_here)
    picker = jnp.arange(RB)[None, :] == my_offsets[:, None]
    pick_half = picker.astype(jnp.bfloat16)
    stride_rows = rows_total // RB

    def strided(matrix):
        return jnp.einsum(
            "arhd,hr->ahd",
            matrix.reshape(stride_rows, RB, heads_here, HS),
            pick_half,
            preferred_element_type=jnp.float32,
        ).astype(jnp.bfloat16)

    far_q = strided(queries)
    far_k = strided(keys_here)
    far_v = strided(values_here)
    piece_k = lax.all_gather(far_k, "seq", axis=0, tiled=True)
    piece_v = lax.all_gather(far_v, "seq", axis=0, tiled=True)
    far_scores = (
        jnp.einsum("ahd,bhd->hab", far_q, piece_k, preferred_element_type=jnp.float32) * score_scale
    )
    far_weights = jnp.exp(far_scores)
    far_add = jnp.einsum(
        "hab,bhd->had",
        far_weights.astype(jnp.bfloat16),
        piece_v,
        preferred_element_type=jnp.float32,
    )
    far_den = jnp.sum(far_weights, axis=-1)
    pick_full = picker.astype(jnp.float32)
    far_num_full = (far_add[:, :, None, :] * pick_full[:, None, :, None]).reshape(
        heads_here, rows_total, HS
    )
    far_den_full = (far_den[:, :, None] * pick_full[:, None, :]).reshape(heads_here, rows_total)
    attended = ((local_num + far_num_full) / (local_den + far_den_full)[:, :, None]).astype(
        jnp.bfloat16
    )
    merged = jnp.transpose(attended, (1, 0, 2)).reshape(rows_total, heads_here * HS)
    partial_out = jnp.dot(merged, w_out, preferred_element_type=jnp.float32)
    summed = lax.psum_scatter(partial_out, "section", scatter_dimension=1, tiled=True)
    width_part = summed.shape[1]
    residual = lax.dynamic_slice_in_dim(x_rows, section_idx * width_part, width_part, 1)
    return (residual.astype(jnp.float32) + summed).astype(jnp.bfloat16)


def solution(mesh):
    placed = (
        P(("section", "seq"), None, None, None),
        P(),
        P(),
        P(),
        P("section", None),
        P("section"),
        P("section", None),
        P(),
        P(),
        P(),
        P(None, "section"),
        P(("section", "seq"), None),
        P(("section", "seq")),
        P(("section", "seq")),
        P("section", None),
        P(),
        P(None, "section"),
        P(),
        P(),
        P(),
        P("section", None),
    )
    return jax.shard_map(
        shards, mesh=mesh, in_specs=placed, out_specs=P("seq", "section"), check_vma=False
    )
```

profile of v0, /device:TPU:8, one launch (start us, length us, event | category | flops | bytes accessed | tf_op | source)
XLA Modules:
  0.0 420.6 jit_solution(15630676997760096784)
XLA Ops:
  6.5 0.7 all-gather.6.cloned.1.call-update
  7.3 0.7 all-gather.8.cloned.1.call-update
  8.1 0.7 all-gather.10.cloned.1.call-update
  10.2 0.8 sub.50
  11.0 19.5 %all-to-all-start = ((s32[128,1,2]{2,1,0:T(1,128)}), s32[128,1,2]{2,1,0:T(1,128)S(1)}, u32[]{:S(2)}, u32[]{:S(2)}) async-start(s32[128,1,2]{2,1,0:T(1,128)} %bitcast.5), calls=%async_computation | async-start | bytes 131072 | tf_op jit(solution)/shard_map/all_to_all | solution.py:117
  32.2 9.5 %fusion.199 = (f32[8,8,8]{2,1,0:T(8,128)S(1)}, f32[8,8,8,768]{3,2,1,0:T(8,128)S(1)}) fusion(f32[768]{0:T(1024)S(1)} %get-tuple-element.54, f32[768]{0:T(1024)S(1)} %get-tuple-element.55, f32[768]{0:T(1024)S(1)} %get-tuple-element.8, f32[768]{0:T(1024)S(1)} %get-tuple-element.9, f32[768]{0:T(1024)S(1)} %get-tuple-element.10, f32[768]{0:T(1024)S(1)} %get-tuple-element.11, ...), kind=kLoop, calls=%fused_computation.360 | loop fusion | flops 38927872 | bytes 3301376 | tf_op jit(solution)/shard_map/reduce_sum | solution.py:13
  42.4 11.2 %all-gather = bf16[4,1,384]{2,1,0:T(2,128)(2,1)S(1)} all-gather(bf16[1,1,384]{2,1,0:T(2,128)(2,1)S(1)} %reshape.264), channel_id=1, replica_groups=mesh['section'=4,'seq'=128] {'section'}, dimensions={0}, use_global_device_ids=true | all-gather | bytes 3840 | tf_op jit(solution)/shard_map/all_gather | solution.py:81
  53.8 0.8 all-gather.6.cloned.1.call-done
  54.6 42.8 %all-gather.8.cloned.1.call-done = bf16[1536,768]{1,0:T(8,128)(2,1)} async-done(((bf16[384,768]{1,0:T(8,128)(2,1)}), bf16[1536,768]{1,0:T(8,128)(2,1)}) %all-gather.8.cloned.1.call-update) | async-done | bytes 2359312 | tf_op jit(solution)/shard_map/all_gather | solution.py:82
  97.5 11.2 %bitcast_reduce_fusion = f32[8,768]{1,0:T(8,128)S(1)} fusion(bf16[1536,768]{1,0:T(8,128)(2,1)} %all-gather.8.cloned.1.call-done, bf16[512,768]{1,0:T(8,128)(2,1)S(1)} %bitcast.95, bf16[1536,768]{1,0:T(8,128)(2,1)} %all-gather.6.cloned.1.call-done, f32[1536]{0:T(1024)S(1)} %reshape.266), kind=kOutput, calls=%fused_computation.170 | convolution fusion | flops 2468210688 | bytes 5535744 | tf_op jit(solution)/shard_map/dot_general | solution.py:47
  109.0 31.4 %all-gather.10.cloned.1.call-done = bf16[768,1536]{1,0:T(8,128)(2,1)} async-done(((bf16[768,384]{1,0:T(8,128)(2,1)}), bf16[768,1536]{1,0:T(8,128)(2,1)}) %all-gather.10.cloned.1.call-update) | async-done | bytes 2359312 | tf_op jit(solution)/shard_map/all_gather | solution.py:83
  140.5 2.1 convolution_convert_fusion.2
  143.1 1.2 reshape.255
  144.3 16.5 %all-to-all-start.1 = ((bf16[128,2,1536]{2,1,0:T(2,128)(2,1)}), bf16[128,2,1536]{2,1,0:T(2,128)(2,1)S(1)}, u32[]{:S(2)}, u32[]{:S(2)}) async-start(bf16[128,2,1536]{2,1,0:T(2,128)(2,1)} %reshape.255), calls=%async_computation.1 | async-start | bytes 1572864 | tf_op jit(solution)/shard_map/all_to_all | solution.py:108
  161.9 0.8 reduce.103
  162.8 39.8 %all-to-all-done.1 = bf16[128,2,1536]{2,1,0:T(2,128)(2,1)S(1)} async-done(((bf16[128,2,1536]{2,1,0:T(2,128)(2,1)}), bf16[128,2,1536]{2,1,0:T(2,128)(2,1)S(1)}, u32[]{:S(2)}, u32[]{:S(2)}) %all-to-all-start.1) | async-done | bytes 786464 | tf_op jit(solution)/shard_map/all_to_all | solution.py:108
  202.9 2.3 fusion.112
  205.3 13.0 %all_gather.29 = bf16[256,768]{1,0:T(8,128)(2,1)S(1)} all-gather(bf16[64,768]{1,0:T(8,128)(2,1)S(1)} %fusion.112), channel_id=1, replica_groups=mesh['section'=4,'seq'=128] {'section'}, dimensions={0}, use_global_device_ids=true | all-gather | bytes 491520 | tf_op jit(solution)/shard_map/all_gather | solution.py:129
  220.1 83.1 %all_gather.30 = bf16[2048,3,64]{2,0,1:T(8,128)(2,1)S(1)} all-gather(bf16[16,3,64]{2,0,1:T(8,128)(2,1)S(1)} %convert_bitcast_fusion.1), channel_id=1, replica_groups=mesh['section'=4,'seq'=128] {'seq'}, dimensions={0}, use_global_device_ids=true | all-gather | bytes 792576 | tf_op jit(solution)/shard_map/all_gather | solution.py:170
  305.0 83.0 %all_gather.31 = bf16[2048,3,64]{2,0,1:T(8,128)(2,1)S(1)} all-gather(bf16[16,3,64]{2,0,1:T(8,128)(2,1)S(1)} %convert_bitcast_fusion), channel_id=1, replica_groups=mesh['section'=4,'seq'=128] {'seq'}, dimensions={0}, use_global_device_ids=true | all-gather | bytes 792576 | tf_op jit(solution)/shard_map/all_gather | solution.py:171
  389.0 1.2 convolution_bitcast_fusion
  390.2 22.0 %reduce-scatter.4.cloned.1.call-done = f32[192,256]{1,0:T(8,128)} async-done(((f32[768,256]{1,0:T(8,128)}), f32[192,256]{1,0:T(8,128)}) %reduce-scatter.4.cloned.1.call-update) | async-done | bytes 196624
  412.2 1.1 copy.62
  413.4 0.7 copy.54
  (108 shorter events, 10.4 us)
Async XLA Ops:
  6.5 212.1 %copy-start = (bf16[768,576]{0,1:T(8,128)(2,1)S(1)}, bf16[768,576]{0,1:T(8,128)(2,1)}, u32[]{:S(2)}) copy-start(bf16[768,576]{0,1:T(8,128)(2,1)} %param.37) | copy-start | bytes 2654212
  6.5 2.9 copy-start.9
  6.5 48.1 %all-gather.6.cloned.1.call-start = ((), (), s32[]{:S(2)}) async-start(), calls=%async_computation.3 | async-start | bytes 2949120 | tf_op jit(solution)/shard_map/all_gather | solution.py:80
  7.3 23.8 %copy-start.3 = (f32[7,7,768]{2,1,0:T(8,128)S(1)}, f32[7,7,768]{2,1,0:T(8,128)}, u32[]{:S(2)}) copy-start(f32[7,7,768]{2,1,0:T(8,128)} %param.22) | copy-start | bytes 451588
  7.3 24.2 %copy-start.1 = (bf16[8,8,8,768]{3,2,1,0:T(8,128)(2,1)S(1)}, bf16[8,8,8,768]{3,2,1,0:T(8,128)(2,1)}, u32[]{:S(2)}) copy-start(bf16[8,8,8,768]{3,2,1,0:T(8,128)(2,1)} %param.21) | copy-start | bytes 2359300
  7.3 90.2 %all-gather.8.cloned.1.call-start = ((), (), s32[]{:S(2)}) async-start(), calls=%async_computation.4 | async-start | bytes 2949120 | tf_op jit(solution)/shard_map/all_gather | solution.py:82
  8.0 132.4 %all-gather.10.cloned.1.call-start = ((), (), s32[]{:S(2)}) async-start(), calls=%async_computation.5 | async-start | bytes 2949120 | tf_op jit(solution)/shard_map/all_gather | solution.py:83
  11.0 133.3 %all-to-all-start = ((s32[128,1,2]{2,1,0:T(1,128)}), s32[128,1,2]{2,1,0:T(1,128)S(1)}, u32[]{:S(2)}, u32[]{:S(2)}) async-start(s32[128,1,2]{2,1,0:T(1,128)} %bitcast.5), calls=%async_computation | async-start | bytes 131072 | tf_op jit(solution)/shard_map/all_to_all | solution.py:117
  30.5 172.5 %all-gather.12.cloned.1.call-start = ((), (), s32[]{:S(2)}) async-start(), calls=%async_computation.6 | async-start | bytes 2949120 | tf_op jit(solution)/shard_map/all_gather | solution.py:84
  31.5 0.7 copy-start.4
  41.7 0.7 copy-start.10
  41.7 11.9 %copy-start.5 = (f32[768]{0:T(1024)S(1)}, f32[768]{0:T(1024)}, u32[]{:S(2)}) copy-start(f32[768]{0:T(1024)} %param.24) | copy-start | bytes 9220
  97.5 11.2 %copy-start.7 = (f32[768]{0:T(1024)S(1)}, f32[768]{0:T(1024)}, u32[]{:S(2)}) copy-start(f32[768]{0:T(1024)} %param.28) | copy-start | bytes 9220
  97.5 11.2 %copy-start.8 = (f32[768]{0:T(1024)S(1)}, f32[768]{0:T(1024)}, u32[]{:S(2)}) copy-start(f32[768]{0:T(1024)} %param.29) | copy-start | bytes 9220
  97.5 43.0 %copy-start.6 = (f32[768]{0:T(1024)S(1)}, f32[768]{0:T(1024)}, u32[]{:S(2)}) copy-start(f32[768]{0:T(1024)} %param.30) | copy-start | bytes 9220
  108.7 33.9 %copy-start.13 = (bf16[152,1536]{1,0:T(8,128)(2,1)S(1)}, bf16[152,1536]{1,0:T(8,128)(2,1)}, u32[]{:S(2)}) copy-start(bf16[152,1536]{1,0:T(8,128)(2,1)} %param.32) | copy-start | bytes 1400836
  143.1 18.0 %copy-start.15 = (s32[12]{0:T(128)S(1)}, s32[12]{0:T(128)}, u32[]{:S(2)}) copy-start(s32[12]{0:T(128)} %param.40) | copy-start | bytes 148
  144.3 58.3 %all-to-all-start.1 = ((bf16[128,2,1536]{2,1,0:T(2,128)(2,1)}), bf16[128,2,1536]{2,1,0:T(2,128)(2,1)S(1)}, u32[]{:S(2)}, u32[]{:S(2)}) async-start(bf16[128,2,1536]{2,1,0:T(2,128)(2,1)} %reshape.255), calls=%async_computation.1 | async-start | bytes 1572864 | tf_op jit(solution)/shard_map/all_to_all | solution.py:108
  160.8 251.4 %reduce-scatter.4.cloned.1.call-start = ((), (), s32[]{:S(2)}) async-start(), calls=%async_computation.7 | async-start | bytes 983040
  202.9 15.7 %copy-start.14 = (f32[768]{0:T(1024)S(1)}, f32[768]{0:T(1024)}, u32[]{:S(2)}) copy-start(f32[768]{0:T(1024)} %param.36) | copy-start | bytes 9220
  219.2 0.7 copy-start.11
  219.3 83.9 %copy-start.12 = (f32[64]{0:T(128)S(1)}, f32[64]{0:T(128)}, u32[]{:S(2)}) copy-start(f32[64]{0:T(128)} %param.38) | copy-start | bytes 772
  388.0 1.0 copy-start.2
Sparse Core Ops, SparseCore 0:
  9.5 45.1 all-gather.5
  56.7 40.7 all-gather.7
  99.6 40.8 all-gather.9
  142.4 40.8 all-gather.11
  390.3 21.8 reduce-scatter.3
where the time goes:
time: 421 us
  blocking collectives  190 us (45%)
  waiting for transfers between devices  140 us (33%)
  starting transfers between devices  36.4 us (9%)
  matrix products  20.1 us (5%)
  between operations  14.2 us (3%)
  other arithmetic  12.9 us (3%)
  local copies, waits for them, and re-layouts  7.37 us (2%)
    all_gather x1, blocking collectives, shards(): piece_k = lax.all_gather(far_k, 'seq', axis=0, tiled=True)  83.1 us
    all_gather x1, blocking collectives, shards(): piece_v = lax.all_gather(far_v, 'seq', axis=0, tiled=True)  83 us
    all_gather x1, waiting for transfers between devices, shards(): lax.all_gather(w_down, 'section', axis=0, tiled=True)  42.8 us
    all_to_all x1, waiting for transfers between devices, shards(): lax.all_to_all(jnp.dot(select_mat, slot_rows, preferred_element_type=jnp....  39.8 us
    all_gather x1, waiting for transfers between devices, shards(): lax.all_gather(w_head, 'section', axis=1, tiled=True)  31.4 us
    unnamed x6, waiting for transfers between devices  24.6 us
    all_to_all x1, starting transfers between devices, shards(): lax.all_to_all(send_rows, 'seq', split_axis=0, concat_axis=0, tiled=True)  19.5 us
    all_to_all x1, starting transfers between devices, shards(): lax.all_to_all(jnp.dot(select_mat, slot_rows, preferred_element_type=jnp....  16.5 us
  transfers between devices with their start and end apart: 7, of which 5 were waited for; matrix products, arithmetic and copies ran while one was open for 7% of the time, Pallas kernels for 0%

commit v1 on v0

--- a/solution.py
+++ b/solution.py
@@ -167,8 +167,11 @@
     far_q = strided(queries)
     far_k = strided(keys_here)
     far_v = strided(values_here)
-    piece_k = lax.all_gather(far_k, "seq", axis=0, tiled=True)
-    piece_v = lax.all_gather(far_v, "seq", axis=0, tiled=True)
+    piece_k, piece_v = jnp.split(
+        lax.all_gather(jnp.concatenate([far_k, far_v], axis=1), "seq", axis=0, tiled=True),
+        [far_k.shape[1]],
+        axis=1,
+    )
     far_scores = (
         jnp.einsum("ahd,bhd->hab", far_q, piece_k, preferred_element_type=jnp.float32) * score_scale
     )

time: 421 us -> 390 us (0.926)
  blocking collectives: 190 us -> 24.1 us
  waiting for transfers between devices: 140 us -> 271 us
    all_gather x2 -> x0, blocking collectives: 166 us -> none  [the longest x1 83.1 us: shards(): piece_k = lax.all_gather(far_k, 'seq', axis=0, tiled=True)]
    all_gather x0 -> x1, waiting for transfers between devices: none -> 127 us  [shards(): lax.all_gather(jnp.concatenate([far_k, far_v], axis=1), 'seq', axis=0, ti...]
    unnamed x6 -> x7, waiting for transfers between devices: 24.6 us -> 28.7 us
  transfers between devices with their start and end apart: 7 -> 8, of which waited for: 5 -> 6; matrix products, arithmetic and copies ran while one was open for 7% -> 8% of each run, Pallas kernels for 0% -> 0%
where the time goes in v1:
time: 390 us; the launch traced here: 389 us
  waiting for transfers between devices  271 us (69%)
  starting transfers between devices  36.4 us (9%)
  blocking collectives  24.1 us (6%)
  matrix products  23 us (6%)
  between operations  14.6 us (4%)
  other arithmetic  13.5 us (3%)
  local copies, waits for them, and re-layouts  7.14 us (2%)
    all_gather x1, waiting for transfers between devices, shards(): lax.all_gather(jnp.concatenate([far_k, far_v], axis=1), 'seq', axis=0, ti...  127 us
    all_gather x1, waiting for transfers between devices, shards(): lax.all_gather(w_down, 'section', axis=0, tiled=True)  42.8 us
    all_to_all x1, waiting for transfers between devices, shards(): lax.all_to_all(jnp.dot(select_mat, slot_rows, preferred_element_type=jnp....  39.9 us
    all_gather x1, waiting for transfers between devices, shards(): lax.all_gather(w_head, 'section', axis=1, tiled=True)  31.4 us
    unnamed x7, waiting for transfers between devices  28.7 us
    all_to_all x1, starting transfers between devices, shards(): lax.all_to_all(send_rows, 'seq', split_axis=0, concat_axis=0, tiled=True)  19.5 us
    all_to_all x1, starting transfers between devices, shards(): lax.all_to_all(jnp.dot(select_mat, slot_rows, preferred_element_type=jnp....  16.5 us
    all_gather x1, blocking collectives, shards(): x_rows = lax.all_gather(x_local, 'section', axis=0, tiled=True)  13 us
  transfers between devices with their start and end apart: 8, of which 6 were waited for; matrix products, arithmetic and copies ran while one was open for 8% of the time, Pallas kernels for 0%

profile of v1, /device:TPU:8, one launch (start us, length us, event | category | flops | bytes accessed | tf_op | source)
XLA Modules:
  0.0 389.3 jit_solution(4346700646325529707)
XLA Ops:
  6.5 0.7 all-gather.7.cloned.1.call-update
  7.3 0.7 all-gather.9.cloned.1.call-update
  10.2 0.8 sub.50
  11.0 19.5 %all-to-all-start = ((s32[128,1,2]{2,1,0:T(1,128)}), s32[128,1,2]{2,1,0:T(1,128)S(1)}, u32[]{:S(2)}, u32[]{:S(2)}) async-start(s32[128,1,2]{2,1,0:T(1,128)} %bitcast.5), calls=%async_computation | async-start | bytes 131072 | tf_op jit(solution)/shard_map/all_to_all | solution.py:117
  32.2 9.5 %fusion.201 = (f32[8,8,8]{2,1,0:T(8,128)S(1)}, f32[8,8,8,768]{3,2,1,0:T(8,128)S(1)}) fusion(f32[768]{0:T(1024)S(1)} %get-tuple-element.54, f32[768]{0:T(1024)S(1)} %get-tuple-element.55, f32[768]{0:T(1024)S(1)} %get-tuple-element.8, f32[768]{0:T(1024)S(1)} %get-tuple-element.9, f32[768]{0:T(1024)S(1)} %get-tuple-element.10, f32[768]{0:T(1024)S(1)} %get-tuple-element.11, ...), kind=kLoop, calls=%fused_computation.363 | loop fusion | flops 38927872 | bytes 3301376 | tf_op jit(solution)/shard_map/reduce_sum | solution.py:13
  42.4 11.2 %all-gather = bf16[4,1,384]{2,1,0:T(2,128)(2,1)S(1)} all-gather(bf16[1,1,384]{2,1,0:T(2,128)(2,1)S(1)} %reshape.264), channel_id=1, replica_groups=mesh['section'=4,'seq'=128] {'section'}, dimensions={0}, use_global_device_ids=true | all-gather | bytes 3840 | tf_op jit(solution)/shard_map/all_gather | solution.py:81
  53.8 0.8 all-gather.7.cloned.1.call-done
  54.6 42.8 %all-gather.9.cloned.1.call-done = bf16[1536,768]{1,0:T(8,128)(2,1)} async-done(((bf16[384,768]{1,0:T(8,128)(2,1)}), bf16[1536,768]{1,0:T(8,128)(2,1)}) %all-gather.9.cloned.1.call-update) | async-done | bytes 2359312 | tf_op jit(solution)/shard_map/all_gather | solution.py:82
  97.5 11.2 %bitcast_reduce_fusion = f32[8,768]{1,0:T(8,128)S(1)} fusion(bf16[1536,768]{1,0:T(8,128)(2,1)} %all-gather.9.cloned.1.call-done, bf16[512,768]{1,0:T(8,128)(2,1)S(1)} %bitcast.93, bf16[1536,768]{1,0:T(8,128)(2,1)} %all-gather.7.cloned.1.call-done, f32[1536]{0:T(1024)S(1)} %reshape.266), kind=kOutput, calls=%fused_computation.173 | convolution fusion | flops 2468210688 | bytes 5535744 | tf_op jit(solution)/shard_map/dot_general | solution.py:47
  109.0 31.4 %all-gather.11.cloned.1.call-done = bf16[768,1536]{1,0:T(8,128)(2,1)} async-done(((bf16[768,384]{1,0:T(8,128)(2,1)}), bf16[768,1536]{1,0:T(8,128)(2,1)}) %all-gather.11.cloned.1.call-update) | async-done | bytes 2359312 | tf_op jit(solution)/shard_map/all_gather | solution.py:83
  140.5 2.1 convolution_convert_fusion.2
  143.1 1.2 reshape.255
  144.3 16.5 %all-to-all-start.1 = ((bf16[128,2,1536]{2,1,0:T(2,128)(2,1)}), bf16[128,2,1536]{2,1,0:T(2,128)(2,1)S(1)}, u32[]{:S(2)}, u32[]{:S(2)}) async-start(bf16[128,2,1536]{2,1,0:T(2,128)(2,1)} %reshape.255), calls=%async_computation.1 | async-start | bytes 1572864 | tf_op jit(solution)/shard_map/all_to_all | solution.py:108
  161.8 0.8 reduce.103
  162.7 39.9 %all-to-all-done.1 = bf16[128,2,1536]{2,1,0:T(2,128)(2,1)S(1)} async-done(((bf16[128,2,1536]{2,1,0:T(2,128)(2,1)}), bf16[128,2,1536]{2,1,0:T(2,128)(2,1)S(1)}, u32[]{:S(2)}, u32[]{:S(2)}) %all-to-all-start.1) | async-done | bytes 786464 | tf_op jit(solution)/shard_map/all_to_all | solution.py:108
  202.9 2.3 fusion.115
  205.3 13.0 %all_gather.26 = bf16[256,768]{1,0:T(8,128)(2,1)S(1)} all-gather(bf16[64,768]{1,0:T(8,128)(2,1)S(1)} %fusion.115), channel_id=1, replica_groups=mesh['section'=4,'seq'=128] {'section'}, dimensions={0}, use_global_device_ids=true | all-gather | bytes 491520 | tf_op jit(solution)/shard_map/all_gather | solution.py:129
  222.0 126.9 %all-gather.15.cloned.1.call-done = bf16[2048,6,64]{2,0,1:T(8,128)(2,1)} async-done(((bf16[16,6,64]{2,0,1:T(8,128)(2,1)}), bf16[2048,6,64]{2,0,1:T(8,128)(2,1)}) %all-gather.15.cloned.1.call-update) | async-done | bytes 1572880 | tf_op jit(solution)/shard_map/all_gather | solution.py:171
  348.8 2.0 fusion.204
  351.0 1.8 fusion.108
  353.2 1.2 convolution_bitcast_fusion
  354.5 26.1 %reduce-scatter.4.cloned.1.call-done = f32[192,256]{1,0:T(8,128)} async-done(((f32[768,256]{1,0:T(8,128)}), f32[192,256]{1,0:T(8,128)}) %reduce-scatter.4.cloned.1.call-update) | async-done | bytes 196624
  380.5 1.1 copy.66
  381.7 0.7 copy.58
  (110 shorter events, 10.7 us)
Async XLA Ops:
  6.5 212.1 %copy-start = (bf16[768,576]{0,1:T(8,128)(2,1)S(1)}, bf16[768,576]{0,1:T(8,128)(2,1)}, u32[]{:S(2)}) copy-start(bf16[768,576]{0,1:T(8,128)(2,1)} %param.37) | copy-start | bytes 2654212
  6.5 2.9 copy-start.9
  6.5 48.1 %all-gather.7.cloned.1.call-start = ((), (), s32[]{:S(2)}) async-start(), calls=%async_computation.3 | async-start | bytes 2949120 | tf_op jit(solution)/shard_map/all_gather | solution.py:80
  7.3 23.8 %copy-start.3 = (f32[7,7,768]{2,1,0:T(8,128)S(1)}, f32[7,7,768]{2,1,0:T(8,128)}, u32[]{:S(2)}) copy-start(f32[7,7,768]{2,1,0:T(8,128)} %param.22) | copy-start | bytes 451588
  7.3 24.2 %copy-start.1 = (bf16[8,8,8,768]{3,2,1,0:T(8,128)(2,1)S(1)}, bf16[8,8,8,768]{3,2,1,0:T(8,128)(2,1)}, u32[]{:S(2)}) copy-start(bf16[8,8,8,768]{3,2,1,0:T(8,128)(2,1)} %param.21) | copy-start | bytes 2359300
  7.3 90.2 %all-gather.9.cloned.1.call-start = ((), (), s32[]{:S(2)}) async-start(), calls=%async_computation.4 | async-start | bytes 2949120 | tf_op jit(solution)/shard_map/all_gather | solution.py:82
  8.0 132.4 %all-gather.11.cloned.1.call-start = ((), (), s32[]{:S(2)}) async-start(), calls=%async_computation.5 | async-start | bytes 2949120 | tf_op jit(solution)/shard_map/all_gather | solution.py:83
  11.0 133.3 %all-to-all-start = ((s32[128,1,2]{2,1,0:T(1,128)}), s32[128,1,2]{2,1,0:T(1,128)S(1)}, u32[]{:S(2)}, u32[]{:S(2)}) async-start(s32[128,1,2]{2,1,0:T(1,128)} %bitcast.5), calls=%async_computation | async-start | bytes 131072 | tf_op jit(solution)/shard_map/all_to_all | solution.py:117
  30.5 172.5 %all-gather.13.cloned.1.call-start = ((), (), s32[]{:S(2)}) async-start(), calls=%async_computation.6 | async-start | bytes 2949120 | tf_op jit(solution)/shard_map/all_gather | solution.py:84
  31.5 0.7 copy-start.4
  41.7 0.7 copy-start.10
  41.7 11.9 %copy-start.5 = (f32[768]{0:T(1024)S(1)}, f32[768]{0:T(1024)}, u32[]{:S(2)}) copy-start(f32[768]{0:T(1024)} %param.24) | copy-start | bytes 9220
  97.5 11.2 %copy-start.7 = (f32[768]{0:T(1024)S(1)}, f32[768]{0:T(1024)}, u32[]{:S(2)}) copy-start(f32[768]{0:T(1024)} %param.28) | copy-start | bytes 9220
  97.5 11.2 %copy-start.8 = (f32[768]{0:T(1024)S(1)}, f32[768]{0:T(1024)}, u32[]{:S(2)}) copy-start(f32[768]{0:T(1024)} %param.29) | copy-start | bytes 9220
  97.5 43.0 %copy-start.6 = (f32[768]{0:T(1024)S(1)}, f32[768]{0:T(1024)}, u32[]{:S(2)}) copy-start(f32[768]{0:T(1024)} %param.30) | copy-start | bytes 9220
  108.7 33.9 %copy-start.13 = (bf16[152,1536]{1,0:T(8,128)(2,1)S(1)}, bf16[152,1536]{1,0:T(8,128)(2,1)}, u32[]{:S(2)}) copy-start(bf16[152,1536]{1,0:T(8,128)(2,1)} %param.32) | copy-start | bytes 1400836
  143.1 18.0 %copy-start.15 = (s32[12]{0:T(128)S(1)}, s32[12]{0:T(128)}, u32[]{:S(2)}) copy-start(s32[12]{0:T(128)} %param.40) | copy-start | bytes 148
  144.3 58.3 %all-to-all-start.1 = ((bf16[128,2,1536]{2,1,0:T(2,128)(2,1)}), bf16[128,2,1536]{2,1,0:T(2,128)(2,1)S(1)}, u32[]{:S(2)}, u32[]{:S(2)}) async-start(bf16[128,2,1536]{2,1,0:T(2,128)(2,1)} %reshape.255), calls=%async_computation.1 | async-start | bytes 1572864 | tf_op jit(solution)/shard_map/all_to_all | solution.py:108
  160.8 188.0 %all-gather.15.cloned.1.call-start = ((), (), s32[]{:S(2)}) async-start(), calls=%async_computation.7 | async-start | bytes 3170304 | tf_op jit(solution)/shard_map/all_gather | solution.py:171
  202.9 15.7 %copy-start.14 = (f32[768]{0:T(1024)S(1)}, f32[768]{0:T(1024)}, u32[]{:S(2)}) copy-start(f32[768]{0:T(1024)} %param.36) | copy-start | bytes 9220
  218.6 0.9 copy-start.11
  219.2 2.1 copy-start.12
  220.9 159.7 %reduce-scatter.4.cloned.1.call-start = ((), (), s32[]{:S(2)}) async-start(), calls=%async_computation.8 | async-start | bytes 983040
  351.0 2.2 copy-start.2
Sparse Core Ops, SparseCore 0:
  9.5 45.1 all-gather.6
  56.7 40.7 all-gather.8
  99.6 40.8 all-gather.10
  142.4 40.8 all-gather.12
  221.0 127.8 all-gather.14
  354.6 25.8 reduce-scatter.3
